TPU v7x, 256 devices: a whole 4x4x8 slice. The times are simulated.
256 devices in a mesh: row: 8 (over z_lo, y), col: 32 (over z_hi, x, core).
Axes of the slice: x: 4, y: 4, z: 8 (z_hi: 4, z_lo: 2; z = z_hi * 2 + z_lo), core: 2. Of those that a mesh axis runs over, the one named last changes fastest.
Arguments:
- tokens: bfloat16 [512, 12288], P('col', 'row'), may hold values from -6 to 6
- grad_out: bfloat16 [512, 12288], P('col', 'row'), may hold values from -6 to 6
- weight_in: bfloat16 [12288, 24576], P('row', 'col'), may hold values from -0.0546875 to 0.0546875
- weight_out: bfloat16 [24576, 12288], P('col', 'row'), may hold values from -0.0390625 to 0.0390625
Outputs:
- output: bfloat16 [512, 12288], P('col', 'row')
- grad_in: bfloat16 [512, 12288], P('col', 'row')
- grad_w_in: bfloat16 [12288, 24576], P('row', 'col')
- grad_w_out: bfloat16 [24576, 12288], P('col', 'row')
All inputs are finite; a program needn't handle non-finite values.
Results may differ from a plain program's by a relative error of at most 0.02.
Values may be sent and summed in bfloat16 or wider, within the bound.
A program may use at most 64 MiB of HBM per device.

v0:
```python
import math
import jax
import jax.numpy as jnp
from jax import lax
from jax.sharding import PartitionSpec as P

root_two_pi = math.sqrt(2.0 / math.pi)


def gelu_value(pre):
    inner = root_two_pi * (pre + 0.044715 * pre * pre * pre)
    return 0.5 * pre * (1.0 + jnp.tanh(inner))


def gelu_slope(pre):
    inner = root_two_pi * (pre + 0.044715 * pre * pre * pre)
    bent = jnp.tanh(inner)
    return 0.5 * (1.0 + bent) + 0.5 * pre * (1.0 - bent * bent) * root_two_pi * (
        1.0 + 3.0 * 0.044715 * pre * pre
    )


def times_transposed(left, right):
    return lax.dot_general(
        left, right, (((1,), (1,)), ((), ())), preferred_element_type=jnp.float32
    )


def inner_tokens(left, right):
    return lax.dot_general(
        left, right, (((0,), (0,)), ((), ())), preferred_element_type=jnp.float32
    )


def shards(tokens, grad_out, weight_in, weight_out):
    token_panel, grad_panel = (
        lax.all_gather(tokens, "col", axis=0, tiled=True),
        lax.all_gather(grad_out, "col", axis=0, tiled=True),
    )
    total_rows = token_panel.shape[0]
    width_hidden = weight_in.shape[1]
    grad_rows = grad_panel
    forward = jnp.dot(token_panel, weight_in, preferred_element_type=jnp.float32)
    backward = times_transposed(grad_rows, weight_out)
    summed = lax.psum_scatter(
        jnp.concatenate([forward, backward], axis=1), "row", scatter_dimension=0, tiled=True
    )
    hidden_pre = summed[:, :width_hidden]
    hidden_act = gelu_value(hidden_pre).astype(jnp.bfloat16)
    pre_grad = (summed[:, width_hidden:] * gelu_slope(hidden_pre)).astype(jnp.bfloat16)
    act_panel, pregrad_panel = (
        lax.all_gather(hidden_act, "row", axis=0, tiled=True),
        lax.all_gather(pre_grad, "row", axis=0, tiled=True),
    )
    factor = 1.0 / math.sqrt(total_rows)
    output = lax.psum_scatter(
        jnp.dot(act_panel, weight_out, preferred_element_type=jnp.float32).astype(jnp.bfloat16),
        "col",
        scatter_dimension=0,
        tiled=True,
    )
    grad_w_out = (inner_tokens(act_panel, grad_panel) * factor).astype(jnp.bfloat16)
    grad_rows = pregrad_panel
    grad_in = lax.psum_scatter(
        times_transposed(grad_rows, weight_in).astype(jnp.bfloat16),
        "col",
        scatter_dimension=0,
        tiled=True,
    )
    grad_w_in = (inner_tokens(token_panel, pregrad_panel) * factor).astype(jnp.bfloat16)
    return (output, grad_in, grad_w_in, grad_w_out)


def solution(mesh):
    placed = (P("col", "row"), P("col", "row"), P("row", "col"), P("col", "row"))
    return jax.shard_map(
        shards,
        mesh=mesh,
        in_specs=placed,
        out_specs=(P("col", "row"), P("col", "row"), P("row", "col"), P("col", "row")),
        check_vma=False,
    )
```

profile of v0, /device:TPU:8, one launch (start us, length us, event | category | flops | bytes accessed | tf_op | source)
XLA Modules:
  0.0 393.0 jit_solution(12617767968671838270)
XLA Ops:
  7.2 0.0 copy-start
  7.2 0.0 all-gather.5.cloned.1.call-start
  7.2 0.7 all-gather.5.cloned.1.call-update
  7.9 0.0 all-gather.3.cloned.1.call-start
  8.0 0.7 all-gather.3.cloned.1.call-update
  8.7 0.0 reduce-scatter.4.cloned.1.call-start
  8.7 57.9 %all-gather.5.cloned.1.call-done = bf16[512,1536]{1,0:T(8,128)(2,1)} async-done(((bf16[16,1536]{1,0:T(8,128)(2,1)}), bf16[512,1536]{1,0:T(8,128)(2,1)}) %all-gather.5.cloned.1.call-update) | async-done | bytes 1572880 | tf_op jit(solution)/shard_map/all_gather | solution.py:38
  66.6 0.0 copy-done
  66.6 4.0 %fusion.9 = f32[512,768]{1,0:T(8,128)} fusion(bf16[512,1536]{1,0:T(8,128)(2,1)} %all-gather.5.cloned.1.call-done, bf16[768,1536]{1,0:T(8,128)(2,1)S(1)} %copy-done), kind=kOutput, calls=%fused_computation.17 | convolution fusion | flops 1207959552 | bytes 5505024 | tf_op jit(solution)/shard_map/dot_general | solution.py:24
  70.6 48.9 %all-gather.3.cloned.1.call-done = bf16[512,1536]{1,0:T(8,128)(2,1)} async-done(((bf16[16,1536]{1,0:T(8,128)(2,1)}), bf16[512,1536]{1,0:T(8,128)(2,1)}) %all-gather.3.cloned.1.call-update) | async-done | bytes 1572880 | tf_op jit(solution)/shard_map/all_gather | solution.py:37
  119.5 0.0 copy-start.1
  119.5 3.6 fusion.8
  123.1 0.0 copy-done.1
  123.1 2.0 pad_maximum_fusion
  125.1 0.0 reduce-scatter.4.cloned.1.call-update
  125.2 0.0 reduce-scatter.6.cloned.1.call-start
  125.2 44.7 %reduce-scatter.4.cloned.1.call-done = f32[64,1536]{1,0:T(8,128)} async-done(((f32[512,1536]{1,0:T(8,128)}), f32[64,1536]{1,0:T(8,128)}) %reduce-scatter.4.cloned.1.call-update) | async-done | bytes 393232 | tf_op jit(solution)/shard_map/reduce_scatter | solution.py:45
  169.9 1.2 fusion.7
  171.1 29.7 %all_gather.14 = bf16[512,768]{1,0:T(8,128)(2,1)S(1)} all-gather(bf16[64,768]{1,0:T(8,128)(2,1)S(1)} %get-tuple-element.9), channel_id=1, replica_groups=mesh['row'=8,'col'=32] {'row'}, dimensions={0}, use_global_device_ids=true | all-gather | bytes 884736 | tf_op jit(solution)/shard_map/all_gather | solution.py:52
  200.8 2.5 convolution_convert_fusion.1
  203.3 0.0 reduce-scatter.6.cloned.1.call-update
  203.3 0.0 reduce-scatter.8.cloned.1.call-start
  203.4 29.7 %all_gather.15 = bf16[512,768]{1,0:T(8,128)(2,1)S(1)} all-gather(bf16[64,768]{1,0:T(8,128)(2,1)S(1)} %get-tuple-element.8), channel_id=1, replica_groups=mesh['row'=8,'col'=32] {'row'}, dimensions={0}, use_global_device_ids=true | all-gather | bytes 884736 | tf_op jit(solution)/shard_map/all_gather | solution.py:53
  233.1 0.0 copy-start.2
  233.1 0.9 copy-done.2
  233.9 4.3 %convolution_convert_fusion = bf16[512,1536]{1,0:T(8,128)(2,1)} fusion(bf16[512,768]{1,0:T(8,128)(2,1)S(1)} %all_gather.15, bf16[1536,768]{1,0:T(8,128)(2,1)} %param.6), kind=kOutput, calls=%fused_computation.4 | convolution fusion | flops 1208745984 | bytes 4718592 | tf_op jit(solution)/shard_map/dot_general | solution.py:24
  238.2 0.0 reduce-scatter.8.cloned.1.call-update
  238.2 4.5 %fusion = bf16[1536,768]{0,1:T(8,128)(2,1)} fusion(bf16[512,768]{1,0:T(8,128)(2,1)} %copy-done.2, bf16[512,1536]{1,0:T(8,128)(2,1)} %all-gather.3.cloned.1.call-done), kind=kOutput, calls=%fused_computation.3 | convolution fusion | flops 1210318848 | bytes 4718592 | tf_op jit(solution)/shard_map/dot_general | solution.py:30
  242.7 4.3 %copy.8 = bf16[1536,768]{1,0:T(8,128)(2,1)} copy(bf16[1536,768]{0,1:T(8,128)(2,1)} %fusion) | data formatting | bytes 4718592
  247.0 4.2 %multiply_convert_fusion = bf16[768,1536]{1,0:T(8,128)(2,1)} fusion(bf16[512,768]{1,0:T(8,128)(2,1)S(1)} %all_gather.14, bf16[512,1536]{1,0:T(8,128)(2,1)} %all-gather.5.cloned.1.call-done), kind=kOutput, calls=%fused_computation | convolution fusion | flops 1210318848 | bytes 4718592 | tf_op jit(solution)/shard_map/dot_general | solution.py:30
  251.2 43.1 %reduce-scatter.6.cloned.1.call-done = bf16[16,1536]{1,0:T(8,128)(2,1)} async-done(((bf16[512,1536]{1,0:T(8,128)(2,1)}), bf16[16,1536]{1,0:T(8,128)(2,1)}) %reduce-scatter.6.cloned.1.call-update) | async-done | bytes 49168 | tf_op jit(solution)/shard_map/reduce_scatter | solution.py:56
  294.4 92.1 %reduce-scatter.8.cloned.1.call-done = bf16[16,1536]{1,0:T(8,128)(2,1)} async-done(((bf16[512,1536]{1,0:T(8,128)(2,1)}), bf16[16,1536]{1,0:T(8,128)(2,1)}) %reduce-scatter.8.cloned.1.call-update) | async-done | bytes 49168 | tf_op jit(solution)/shard_map/reduce_scatter | solution.py:64
Async XLA Ops:
  7.2 59.4 %copy-start = (bf16[768,1536]{1,0:T(8,128)(2,1)S(1)}, bf16[768,1536]{1,0:T(8,128)(2,1)}, u32[]{:S(2)}) copy-start(bf16[768,1536]{1,0:T(8,128)(2,1)} %param.7) | copy-start | bytes 7077892
  7.2 59.4 %all-gather.5.cloned.1.call-start = ((), (), s32[]{:S(2)}) async-start(), calls=%async_computation.4 | async-start | bytes 1622016 | tf_op jit(solution)/shard_map/all_gather | solution.py:38
  7.9 111.6 %all-gather.3.cloned.1.call-start = ((), (), s32[]{:S(2)}) async-start(), calls=%async_computation.3 | async-start | bytes 1622016 | tf_op jit(solution)/shard_map/all_gather | solution.py:37
  8.7 161.2 %reduce-scatter.4.cloned.1.call-start = ((), (), s32[]{:S(2)}) async-start(), calls=%async_computation.5 | async-start | bytes 3538944 | tf_op jit(solution)/shard_map/reduce_scatter | solution.py:45
  119.5 3.6 copy-start.1
  125.2 169.2 %reduce-scatter.6.cloned.1.call-start = ((), (), s32[]{:S(2)}) async-start(), calls=%async_computation.6 | async-start | bytes 1622016 | tf_op jit(solution)/shard_map/reduce_scatter | solution.py:56
  203.3 183.1 %reduce-scatter.8.cloned.1.call-start = ((), (), s32[]{:S(2)}) async-start(), calls=%async_computation.7 | async-start | bytes 1622016 | tf_op jit(solution)/shard_map/reduce_scatter | solution.py:64
  233.1 0.9 copy-start.2
Sparse Core Ops, SparseCore 0:
  10.6 55.9 all-gather.4
  69.1 50.2 all-gather.2
  125.3 44.5 reduce-scatter.3
  203.5 90.8 reduce-scatter.5
  298.6 87.7 reduce-scatter.7
where the time goes:
time: 393 us
  waiting for transfers between devices  288 us (73%)
  blocking collectives  59.4 us (15%)
  matrix products  23.1 us (6%)
  between operations  13.8 us (4%)
  local copies, waits for them, and re-layouts  5.16 us (1%)
    reduce_scatter x1, waiting for transfers between devices, shards(): lax.psum_scatter(times_transposed(grad_rows, weight_in).astype(jnp.bfloat...  92.1 us
    all_gather x1, waiting for transfers between devices, shards(): lax.all_gather(grad_out, 'col', axis=0, tiled=True)  57.9 us
    all_gather x1, waiting for transfers between devices, shards(): lax.all_gather(tokens, 'col', axis=0, tiled=True)  48.9 us
    reduce_scatter x1, waiting for transfers between devices, shards(): lax.psum_scatter(jnp.concatenate([forward, backward], axis=1), 'row', sca...  44.7 us
    reduce_scatter x1, waiting for transfers between devices, shards(): lax.psum_scatter(jnp.dot(act_panel, weight_out, preferred_element_type=jn...  43.1 us
    all_gather x1, blocking collectives, shards(): lax.all_gather(hidden_act, 'row', axis=0, tiled=True)  29.7 us
    all_gather x1, blocking collectives, shards(): lax.all_gather(pre_grad, 'row', axis=0, tiled=True)  29.7 us
    dot_general x2, matrix products, inner_tokens(): lax.dot_general(left, right, (((0,), (0,)), ((), ())), preferred_element_...  8.73 us
  transfers between devices with their start and end apart: 5, of which 5 were waited for; matrix products, arithmetic and copies ran while one was open for 5% of the time, Pallas kernels for 0%

commit v1 on v0

--- a/solution.py
+++ b/solution.py
@@ -33,9 +33,15 @@
 
 
 def shards(tokens, grad_out, weight_in, weight_out):
+
+    def _bring_rates(sample, dim_k):
+        inter = lax.all_to_all(jnp.stack(lax.axis_size("col") * [sample], axis=0), "col", 0, 0)
+        tmp = jnp.concatenate(inter, axis=dim_k)
+        return tmp
+
     token_panel, grad_panel = (
         lax.all_gather(tokens, "col", axis=0, tiled=True),
-        lax.all_gather(grad_out, "col", axis=0, tiled=True),
+        _bring_rates(grad_out, 0),
     )
     total_rows = token_panel.shape[0]
     width_hidden = weight_in.shape[1]

time: 393 us -> 359 us (0.913)
  waiting for transfers between devices: 288 us -> 240 us
  starting transfers between devices: 0.2 us -> 11.6 us
    all_gather x1 -> x0, waiting for transfers between devices: 57.9 us -> none  [shards(): lax.all_gather(grad_out, 'col', axis=0, tiled=True)]
    all_to_all x0 -> x1, waiting for transfers between devices: none -> 38.8 us  [_bring_rates(): lax.all_to_all(jnp.stack(lax.axis_size('col') * [sample], axis=0), 'col',...]
    all_gather x1, waiting for transfers between devices: 48.9 us -> 20.8 us  [shards(): lax.all_gather(tokens, 'col', axis=0, tiled=True)]
    all_to_all x0 -> x1, starting transfers between devices: none -> 11.4 us  [_bring_rates(): lax.all_to_all(jnp.stack(lax.axis_size('col') * [sample], axis=0), 'col',...]
  transfers between devices with their start and end apart: 5 -> 5, of which waited for: 5 -> 5; matrix products, arithmetic and copies ran while one was open for 5% -> 6% of each run, Pallas kernels for 0% -> 0%
where the time goes in v1:
time: 359 us
  waiting for transfers between devices  240 us (67%)
  blocking collectives  59.4 us (17%)
  matrix products  23.1 us (6%)
  between operations  13.8 us (4%)
  starting transfers between devices  11.6 us (3%)
  local copies, waits for them, and re-layouts  7.43 us (2%)
    reduce_scatter x1, waiting for transfers between devices, shards(): lax.psum_scatter(times_transposed(grad_rows, weight_in).astype(jnp.bfloat...  92.1 us
    reduce_scatter x1, waiting for transfers between devices, shards(): lax.psum_scatter(jnp.concatenate([forward, backward], axis=1), 'row', sca...  44.7 us
    reduce_scatter x1, waiting for transfers between devices, shards(): lax.psum_scatter(jnp.dot(act_panel, weight_out, preferred_element_type=jn...  43.2 us
    all_to_all x1, waiting for transfers between devices, _bring_rates(): lax.all_to_all(jnp.stack(lax.axis_size('col') * [sample], axis=0), 'col',...  38.8 us
    all_gather x1, blocking collectives, shards(): lax.all_gather(hidden_act, 'row', axis=0, tiled=True)  29.8 us
    all_gather x1, blocking collectives, shards(): lax.all_gather(pre_grad, 'row', axis=0, tiled=True)  29.7 us
    all_gather x1, waiting for transfers between devices, shards(): lax.all_gather(tokens, 'col', axis=0, tiled=True)  20.8 us
    all_to_all x1, starting transfers between devices, _bring_rates(): lax.all_to_all(jnp.stack(lax.axis_size('col') * [sample], axis=0), 'col',...  11.4 us
  transfers between devices with their start and end apart: 5, of which 5 were waited for; matrix products, arithmetic and copies ran while one was open for 6% of the time, Pallas kernels for 0%

profile of v1, /device:TPU:8, one launch (start us, length us, event | category | flops | bytes accessed | tf_op | source)
XLA Modules:
  0.0 358.9 jit_solution(12613587689214695184)
XLA Ops:
  7.2 0.0 copy-start
  7.2 2.3 stack.2
  9.4 11.4 %all-to-all-start = ((bf16[32,16,1536]{2,1,0:T(8,128)(2,1)}), bf16[32,16,1536]{2,1,0:T(8,128)(2,1)}, u32[]{:S(2)}, u32[]{:S(2)}) async-start(bf16[32,16,1536]{2,1,0:T(8,128)(2,1)} %stack.2), calls=%async_computation | async-start | bytes 3145728 | tf_op jit(solution)/shard_map/all_to_all | solution.py:38
  20.9 0.0 all-gather.2.cloned.1.call-start
  20.9 0.7 all-gather.2.cloned.1.call-update
  21.6 0.0 reduce-scatter.4.cloned.1.call-start
  21.7 38.8 %all-to-all-done = bf16[32,16,1536]{2,1,0:T(8,128)(2,1)} async-done(((bf16[32,16,1536]{2,1,0:T(8,128)(2,1)}), bf16[32,16,1536]{2,1,0:T(8,128)(2,1)}, u32[]{:S(2)}, u32[]{:S(2)}) %all-to-all-start) | async-done | bytes 1572896 | tf_op jit(solution)/shard_map/all_to_all | solution.py:38
  60.5 0.0 copy-done
  60.5 4.0 %fusion.9 = f32[512,768]{1,0:T(8,128)} fusion(bf16[512,1536]{1,0:T(8,128)(2,1)} %bitcast, bf16[768,1536]{1,0:T(8,128)(2,1)S(1)} %copy-done), kind=kOutput, calls=%fused_computation.17 | convolution fusion | flops 1207959552 | bytes 5505024 | tf_op jit(solution)/shard_map/dot_general | solution.py:24
  64.4 20.8 %all-gather.2.cloned.1.call-done = bf16[512,1536]{1,0:T(8,128)(2,1)} async-done(((bf16[16,1536]{1,0:T(8,128)(2,1)}), bf16[512,1536]{1,0:T(8,128)(2,1)}) %all-gather.2.cloned.1.call-update) | async-done | bytes 1572880 | tf_op jit(solution)/shard_map/all_gather | solution.py:43
  85.2 0.0 copy-start.1
  85.2 3.6 %fusion.8 = f32[512,768]{1,0:T(8,128)S(1)} fusion(bf16[512,1536]{1,0:T(8,128)(2,1)} %all-gather.2.cloned.1.call-done, bf16[1536,768]{1,0:T(8,128)(2,1)} %param.6), kind=kOutput, calls=%fused_computation.16 | convolution fusion | flops 1207959552 | bytes 5505024 | tf_op jit(solution)/shard_map/dot_general | solution.py:49
  88.8 0.0 copy-done.1
  88.9 2.0 pad_maximum_fusion
  90.9 0.0 reduce-scatter.4.cloned.1.call-update
  90.9 0.0 reduce-scatter.6.cloned.1.call-start
  90.9 44.7 %reduce-scatter.4.cloned.1.call-done = f32[64,1536]{1,0:T(8,128)} async-done(((f32[512,1536]{1,0:T(8,128)}), f32[64,1536]{1,0:T(8,128)}) %reduce-scatter.4.cloned.1.call-update) | async-done | bytes 393232 | tf_op jit(solution)/shard_map/reduce_scatter | solution.py:51
  135.7 1.2 fusion.7
  136.8 29.8 %all_gather.10 = bf16[512,768]{1,0:T(8,128)(2,1)S(1)} all-gather(bf16[64,768]{1,0:T(8,128)(2,1)S(1)} %get-tuple-element.9), channel_id=1, replica_groups=mesh['row'=8,'col'=32] {'row'}, dimensions={0}, use_global_device_ids=true | all-gather | bytes 884736 | tf_op jit(solution)/shard_map/all_gather | solution.py:58
  166.6 2.5 convolution_convert_fusion.1
  169.1 0.0 reduce-scatter.6.cloned.1.call-update
  169.2 0.0 reduce-scatter.8.cloned.1.call-start
  169.2 29.7 %all_gather.11 = bf16[512,768]{1,0:T(8,128)(2,1)S(1)} all-gather(bf16[64,768]{1,0:T(8,128)(2,1)S(1)} %get-tuple-element.8), channel_id=1, replica_groups=mesh['row'=8,'col'=32] {'row'}, dimensions={0}, use_global_device_ids=true | all-gather | bytes 884736 | tf_op jit(solution)/shard_map/all_gather | solution.py:59
  198.9 0.0 copy-start.2
  198.9 0.9 copy-done.2
  199.8 4.3 %convolution_convert_fusion = bf16[512,1536]{1,0:T(8,128)(2,1)} fusion(bf16[512,768]{1,0:T(8,128)(2,1)S(1)} %all_gather.11, bf16[1536,768]{1,0:T(8,128)(2,1)} %param.6), kind=kOutput, calls=%fused_computation.4 | convolution fusion | flops 1208745984 | bytes 4718592 | tf_op jit(solution)/shard_map/dot_general | solution.py:24
  204.0 0.0 reduce-scatter.8.cloned.1.call-update
  204.1 4.5 %fusion = bf16[1536,768]{0,1:T(8,128)(2,1)} fusion(bf16[512,768]{1,0:T(8,128)(2,1)} %copy-done.2, bf16[512,1536]{1,0:T(8,128)(2,1)} %all-gather.2.cloned.1.call-done), kind=kOutput, calls=%fused_computation.3 | convolution fusion | flops 1210318848 | bytes 4718592 | tf_op jit(solution)/shard_map/dot_general | solution.py:30
  208.6 4.3 %copy.8 = bf16[1536,768]{1,0:T(8,128)(2,1)} copy(bf16[1536,768]{0,1:T(8,128)(2,1)} %fusion) | data formatting | bytes 4718592
  212.8 4.2 %multiply_convert_fusion = bf16[768,1536]{1,0:T(8,128)(2,1)} fusion(bf16[512,768]{1,0:T(8,128)(2,1)S(1)} %all_gather.10, bf16[512,1536]{1,0:T(8,128)(2,1)} %bitcast), kind=kOutput, calls=%fused_computation | convolution fusion | flops 1210318848 | bytes 4718592 | tf_op jit(solution)/shard_map/dot_general | solution.py:30
  217.1 43.2 %reduce-scatter.6.cloned.1.call-done = bf16[16,1536]{1,0:T(8,128)(2,1)} async-done(((bf16[512,1536]{1,0:T(8,128)(2,1)}), bf16[16,1536]{1,0:T(8,128)(2,1)}) %reduce-scatter.6.cloned.1.call-update) | async-done | bytes 49168 | tf_op jit(solution)/shard_map/reduce_scatter | solution.py:62
  260.3 92.1 %reduce-scatter.8.cloned.1.call-done = bf16[16,1536]{1,0:T(8,128)(2,1)} async-done(((bf16[512,1536]{1,0:T(8,128)(2,1)}), bf16[16,1536]{1,0:T(8,128)(2,1)}) %reduce-scatter.8.cloned.1.call-update) | async-done | bytes 49168 | tf_op jit(solution)/shard_map/reduce_scatter | solution.py:70
Async XLA Ops:
  7.2 53.3 %copy-start = (bf16[768,1536]{1,0:T(8,128)(2,1)S(1)}, bf16[768,1536]{1,0:T(8,128)(2,1)}, u32[]{:S(2)}) copy-start(bf16[768,1536]{1,0:T(8,128)(2,1)} %param.7) | copy-start | bytes 7077892
  9.4 51.0 %all-to-all-start = ((bf16[32,16,1536]{2,1,0:T(8,128)(2,1)}), bf16[32,16,1536]{2,1,0:T(8,128)(2,1)}, u32[]{:S(2)}, u32[]{:S(2)}) async-start(bf16[32,16,1536]{2,1,0:T(8,128)(2,1)} %stack.2), calls=%async_computation | async-start | bytes 3145728 | tf_op jit(solution)/shard_map/all_to_all | solution.py:38
  20.9 64.3 %all-gather.2.cloned.1.call-start = ((), (), s32[]{:S(2)}) async-start(), calls=%async_computation.4 | async-start | bytes 1622016 | tf_op jit(solution)/shard_map/all_gather | solution.py:43
  21.6 114.0 %reduce-scatter.4.cloned.1.call-start = ((), (), s32[]{:S(2)}) async-start(), calls=%async_computation.5 | async-start | bytes 3538944 | tf_op jit(solution)/shard_map/reduce_scatter | solution.py:51
  85.2 3.6 %copy-start.1 = (f32[512,768]{1,0:T(8,128)S(1)}, f32[512,768]{1,0:T(8,128)}, u32[]{:S(2)}) copy-start(f32[512,768]{1,0:T(8,128)} %fusion.9) | copy-start | bytes 4718596
  90.9 169.4 %reduce-scatter.6.cloned.1.call-start = ((), (), s32[]{:S(2)}) async-start(), calls=%async_computation.6 | async-start | bytes 1622016 | tf_op jit(solution)/shard_map/reduce_scatter | solution.py:62
  169.2 183.3 %reduce-scatter.8.cloned.1.call-start = ((), (), s32[]{:S(2)}) async-start(), calls=%async_computation.7 | async-start | bytes 1622016 | tf_op jit(solution)/shard_map/reduce_scatter | solution.py:70
  198.9 0.9 copy-start.2
Sparse Core Ops, SparseCore 0:
  24.3 60.8 all-gather.1
  91.0 44.6 reduce-scatter.3
  169.3 90.9 reduce-scatter.5
  264.6 87.8 reduce-scatter.7
